TPU v7x, 128 devices: a whole 4x4x4 slice. The times are simulated.
128 devices in a mesh: view: 2 (over z_lo), dp: 64 (over y, z_hi, x, core).
Axes of the slice: x: 4, y: 4, z: 4 (z_hi: 2, z_lo: 2; z = z_hi * 2 + z_lo), core: 2. Of those that a mesh axis runs over, the one named last changes fastest.
Arguments:
- hidden: bfloat16 [2, 896, 4096], P('view', 'dp')
- weight: bfloat16 [4096, 8192], P(None, 'dp')
Outputs:
- grad_hidden: float32 [2, 896, 4096], P('view', 'dp')
- grad_weight: float32 [4096, 8192], P(None, 'dp')
All inputs are finite; a program needn't handle non-finite values.
Results may differ from a plain program's by a relative error of at most 0.003.
Values may be sent and summed in bfloat16 or wider, within the bound.
No kernel may reach another device: no remote copies, remote signals or barrier semaphores. Data moves between devices by JAX's collectives and lax.ppermute only.
A program may use at most 128 MiB of HBM per device.

v0:
```python
import jax
import jax.numpy as jnp
from jax import lax
from jax.sharding import PartitionSpec as P


def from_partner(block, axis, apart):
    count = lax.axis_size(axis)
    route = []
    for low in range(count):
        high = low | 1 << apart
        if high != low and high < count:
            route += [(low, high), (high, low)]
    return lax.ppermute(block, axis, route)


def split_parts(values):
    upper = values.astype(jnp.bfloat16)
    lower = (values - upper.astype(jnp.float32)).astype(jnp.bfloat16)
    return (upper, lower)


def coupling_term(centered):
    segment = lax.all_gather(centered, "dp", axis=1, tiled=True)
    product_tile = lax.dot_general(
        centered, segment, (((0,), (0,)), ((), ())), preferred_element_type=jnp.float32
    )
    tile_upper, tile_lower = split_parts(product_tile)
    dims = (((1,), (1,)), ((), ()))
    running = lax.dot_general(segment, tile_upper, dims, preferred_element_type=jnp.float32)
    return running + lax.dot_general(segment, tile_lower, dims, preferred_element_type=jnp.float32)


def view_gradient(embedded, partner, weight):
    total_rows = embedded.shape[0]
    embed_wide = embedded.astype(jnp.float32)
    centered = (embed_wide - jnp.mean(embed_wide, axis=0, keepdims=True)).astype(jnp.bfloat16)
    centered_wide = centered.astype(jnp.float32)
    sum_squares = jnp.sum(centered_wide * centered_wide, axis=0, keepdims=True)
    spread_std = jnp.sqrt(sum_squares / (total_rows - 1) + 0.0001)
    coupled = coupling_term(centered)
    coef_var = total_rows / (2.0 * (total_rows - 1))
    coef_cov = 0.08 * total_rows / ((total_rows - 1) * (total_rows - 1))
    hinge_weight = jax.nn.sigmoid(10.0 * (1.0 - spread_std))
    combined = (
        embed_wide
        - partner.astype(jnp.float32)
        - coef_var * hinge_weight * centered_wide / spread_std
    )
    combined = combined + coef_cov * (coupled - centered_wide * sum_squares)
    grad_embed = combined.astype(jnp.bfloat16)
    grad_rows = lax.psum_scatter(
        lax.dot_general(
            grad_embed, weight, (((1,), (1,)), ((), ())), preferred_element_type=jnp.float32
        ),
        "dp",
        scatter_dimension=0,
        tiled=True,
    )
    return (grad_embed, grad_rows)


def on_device(hidden, weight):
    local_views = hidden.shape[0]
    gathered = lax.all_gather(hidden, "dp", axis=1, tiled=True)
    total_rows = gathered.shape[1]
    in_width = gathered.shape[2]
    flat = gathered.reshape(local_views * total_rows, in_width)
    embedded = jnp.dot(flat, weight, preferred_element_type=jnp.float32).astype(jnp.bfloat16)
    embedded = embedded.reshape(local_views, total_rows, weight.shape[1])
    partners = from_partner(embedded, "view", 0)
    grad_embed, grad_rows = view_gradient(embedded[0], partners[0], weight)
    grad_list = [grad_rows]
    weight_part = lax.dot_general(
        gathered[0], grad_embed, (((0,), (0,)), ((), ())), preferred_element_type=jnp.float32
    )
    grad_weight = lax.psum(weight_part, "view") / jnp.sqrt(2.0 * total_rows)
    return (jnp.stack(grad_list), grad_weight)


def solution(mesh):
    return jax.shard_map(
        on_device,
        mesh=mesh,
        in_specs=(P("view", "dp", None), P(None, "dp")),
        out_specs=(P("view", "dp", None), P(None, "dp")),
        check_vma=False,
    )
```

profile of v0, /device:TPU:8, one launch (start us, length us, event | category | flops | bytes accessed | tf_op | source)
XLA Modules:
  0.0 558.8 jit_solution(7315536405936615213)
XLA Ops:
  7.2 1.9 copy.9
  9.2 105.2 %all-gather.3.cloned.1.call-done = bf16[1,896,4096]{2,0,1:T(2,128)(2,1)} async-done(((bf16[1,14,4096]{2,0,1:T(2,128)(2,1)}), bf16[1,896,4096]{2,0,1:T(2,128)(2,1)}) %all-gather.3.cloned.1.call-update) | async-done | bytes 7340048 | tf_op jit(solution)/shard_map/all_gather | solution.py:65
  114.3 12.9 %convert_reduce_fusion = (f32[128]{0:T(128)S(1)}, bf16[896,128]{1,0:T(8,128)(2,1)S(1)}) fusion(bf16[4096,128]{1,0:T(8,128)(2,1)S(1)} %copy-done, bf16[1,896,4096]{2,0,1:T(2,128)(2,1)} %all-gather.3.cloned.1.call-done), kind=kOutput, calls=%fused_computation.21 | convolution fusion | flops 939868032 | bytes 8618496 | tf_op jit(solution)/shard_map/dot_general | solution.py:69
  129.1 130.5 %all-gather.5.cloned.1.call-done = bf16[896,8192]{1,0:T(8,128)(2,1)} async-done(((bf16[896,128]{1,0:T(8,128)(2,1)}), bf16[896,8192]{1,0:T(8,128)(2,1)}) %all-gather.5.cloned.1.call-update) | async-done | bytes 14680080 | tf_op jit(solution)/shard_map/all_gather | solution.py:24
  259.6 8.0 %fusion.26 = f32[128,8192]{1,0:T(8,128)S(1)} fusion(bf16[896,8192]{1,0:T(8,128)(2,1)} %all-gather.5.cloned.1.call-done, bf16[896,128]{1,0:T(8,128)(2,1)S(1)} %get-tuple-element.13, f32[128]{0:T(128)S(1)} %broadcast_multiply_fusion.1), kind=kOutput, calls=%fused_computation.30 | convolution fusion | flops 1879392256 | bytes 19104256 | tf_op jit(solution)/shard_map/dot_general | solution.py:25
  268.9 3.9 fusion.18
  272.9 4.2 fusion.22
  277.1 7.5 %fusion.28 = f32[896,4096]{1,0:T(8,128)} fusion(bf16[896,128]{1,0:T(8,128)(2,1)S(1)} %fusion.22, bf16[4096,128]{1,0:T(8,128)(2,1)S(1)} %copy-done), kind=kOutput, calls=%fused_computation.34 | convolution fusion | flops 939524096 | bytes 15958016 | tf_op jit(solution)/shard_map/dot_general | solution.py:53
  284.6 14.8 %fusion.5 = f32[4096,128]{0,1:T(8,128)} fusion(bf16[896,128]{1,0:T(8,128)(2,1)S(1)} %fusion.22, bf16[1,896,4096]{2,0,1:T(2,128)(2,1)} %all-gather.3.cloned.1.call-done), kind=kOutput, calls=%fused_computation.4 | convolution fusion | flops 939524096 | bytes 9666560 | tf_op jit(solution)/shard_map/dot_general | solution.py:74
  299.5 171.8 %fusion = f32[16,4096]{1,0:T(8,128)S(1)} fusion(f32[896,4096]{1,0:T(8,128)} %fusion.28), kind=kCustom, calls=%all-reduce-scatter | all-reduce-scatter fusion | flops 4194305 | bytes 14942720
  471.3 1.9 collective-permute-start.1
  473.2 1.9 collective-permute-start.2
  475.2 1.9 collective-permute-start.8
  477.1 1.9 collective-permute-start.3
  479.0 9.9 %collective-permute-start.4 = (f32[16,4096]{1,0:T(8,128)S(1)}, f32[16,4096]{1,0:T(8,128)S(1)}, u32[]{:S(2)}, u32[]{:S(2)}) collective-permute-start(f32[16,4096]{1,0:T(8,128)S(1)} %fusion), channel_id=1, source_target_pairs={{0,4},{1,5},{2,6},{3,7},{4,8},{5,9},{6,10},{7,11},{8,12},{9,13},{1... | collective-permute-start | bytes 786440
  488.9 16.9 %collective-permute-done.8 = f32[14,4096]{1,0:T(8,128)S(1)} collective-permute-done((f32[14,4096]{1,0:T(8,128)S(1)}, f32[14,4096]{1,0:T(8,128)S(1)}, u32[]{:S(2)}, u32[]{:S(2)}) %collective-permute-start.8) | collective-permute-done | bytes 229408
  505.8 1.9 collective-permute-start.5
  507.7 1.9 collective-permute-start.6
  509.7 1.9 collective-permute-start.7
  512.9 6.1 %collective-permute-done.5 = f32[16,4096]{1,0:T(8,128)S(1)} collective-permute-done((f32[16,4096]{1,0:T(8,128)S(1)}, f32[16,4096]{1,0:T(8,128)S(1)}, u32[]{:S(2)}, u32[]{:S(2)}) %collective-permute-start.5) | collective-permute-done | bytes 262176
  519.0 6.1 %collective-permute-done.6 = f32[16,4096]{1,0:T(8,128)S(1)} collective-permute-done((f32[16,4096]{1,0:T(8,128)S(1)}, f32[16,4096]{1,0:T(8,128)S(1)}, u32[]{:S(2)}, u32[]{:S(2)}) %collective-permute-start.6) | collective-permute-done | bytes 262176
  525.8 5.1 collective-permute-done.7
  530.9 16.7 %concatenate = f32[142,4096]{1,0:T(8,128)S(1)} concatenate(f32[14,4096]{1,0:T(8,128)} %copy-done.5, f32[16,4096]{1,0:T(8,128)} %collective-permute-done.7, f32[16,4096]{1,0:T(8,128)} %copy-done.9, f32[16,4096]{1,0:T(8,128)} %copy-done.8, f32[16,4096]{1,0:T(8,128)} %copy-done.7, f32[16,4096]{1,0:T(8,128)} %copy-done.6, f32[16,4096]{1,0:T(8,128)} %copy-done.4, ...), dimensions={0} | concatenate | bytes 4653056
  550.4 1.8 copy.11
  (43 shorter events, 7.4 us)
Async XLA Ops:
  7.2 107.2 %copy-start = (bf16[4096,128]{1,0:T(8,128)(2,1)S(1)}, bf16[4096,128]{1,0:T(8,128)(2,1)}, u32[]{:S(2)}) copy-start(bf16[4096,128]{1,0:T(8,128)(2,1)} %param.3) | copy-start | bytes 3145732
  7.2 107.2 %all-gather.3.cloned.1.call-start = ((), (), s32[]{:S(2)}) async-start(), calls=%async_computation | async-start | bytes 14909440 | tf_op jit(solution)/shard_map/all_gather | solution.py:65
  9.1 250.5 %all-gather.5.cloned.1.call-start = ((), (), s32[]{:S(2)}) async-start(), calls=%async_computation.1 | async-start | bytes 14909440 | tf_op jit(solution)/shard_map/all_gather | solution.py:24
  128.1 420.6 %all-reduce.4.cloned.1.call-start = ((), (), s32[]{:S(2)}) async-start(), calls=%async_computation.2 | async-start | bytes 4194304 | tf_op jit(solution)/shard_map/psum | solution.py:77
  128.1 144.8 %collective-permute-start = (bf16[1,896,128]{2,1,0:T(8,128)(2,1)S(1)}, bf16[1,896,128]{2,1,0:T(8,128)(2,1)S(1)}, u32[]{:S(2)}, u32[]{:S(2)}) collective-permute-start(bf16[1,896,128]{2,1,0:T(8,128)(2,1)S(1)} %bitcast.29), channel_id=1, source_target_pairs={{0,64},{64,0},{1,65},{65,1},{2,66},{66,2},{3,67},{67,3},{4,68},{68... | collective-permute-start | bytes 688136 | tf_op jit(solution)/shard_map/ppermute | solution.py:14
  259.6 9.3 %copy-start.1 = (bf16[896,8192]{1,0:T(8,128)(2,1)S(1)}, bf16[896,8192]{1,0:T(8,128)(2,1)}, u32[]{:S(2)}) copy-start(bf16[896,8192]{1,0:T(8,128)(2,1)} %all-gather.5.cloned.1.call-done) | copy-start | bytes 44040196
  299.4 212.2 %copy-start.10 = (u32[128]{0:T(128)S(1)}, u32[128]{0:T(128)}, u32[]{:S(2)}) copy-start(u32[128]{0:T(128)} %constant.24) | copy-start | bytes 1540
  471.3 53.8 %copy-start.2 = (f32[16,4096]{1,0:T(8,128)}, f32[16,4096]{1,0:T(8,128)S(1)}, u32[]{:S(2)}) copy-start(f32[16,4096]{1,0:T(8,128)S(1)} %fusion) | copy-start | bytes 786436
  471.3 36.4 %collective-permute-start.1 = (f32[16,4096]{1,0:T(8,128)S(1)}, f32[16,4096]{1,0:T(8,128)S(1)}, u32[]{:S(2)}, u32[]{:S(2)}) collective-permute-start(f32[16,4096]{1,0:T(8,128)S(1)} %fusion), channel_id=1, source_target_pairs={{0,1},{1,2},{2,3},{3,4},{4,5},{5,6},{6,7},{7,8},{8,9},{9,10},{10,1... | collective-permute-start | bytes 786440
  473.2 36.5 %collective-permute-start.2 = (f32[16,4096]{1,0:T(8,128)S(1)}, f32[16,4096]{1,0:T(8,128)S(1)}, u32[]{:S(2)}, u32[]{:S(2)}) collective-permute-start(f32[16,4096]{1,0:T(8,128)S(1)} %fusion), channel_id=1, source_target_pairs={{0,2},{1,3},{2,4},{3,5},{4,6},{5,7},{6,8},{7,9},{8,10},{9,11},{10,... | collective-permute-start | bytes 786440
  475.2 30.6 %collective-permute-start.8 = (f32[14,4096]{1,0:T(8,128)S(1)}, f32[14,4096]{1,0:T(8,128)S(1)}, u32[]{:S(2)}, u32[]{:S(2)}) collective-permute-start(f32[14,4096]{1,0:T(8,128)S(1)} %slice), channel_id=1, source_target_pairs={{0,8},{1,9},{2,10},{3,11},{4,12},{5,13},{6,14},{7,15},{8,16},{9,17... | collective-permute-start | bytes 688136
  477.1 35.8 %collective-permute-start.3 = (f32[16,4096]{1,0:T(8,128)S(1)}, f32[16,4096]{1,0:T(8,128)S(1)}, u32[]{:S(2)}, u32[]{:S(2)}) collective-permute-start(f32[16,4096]{1,0:T(8,128)S(1)} %fusion), channel_id=1, source_target_pairs={{0,3},{1,4},{2,5},{3,6},{4,7},{5,8},{6,9},{7,10},{8,11},{9,12},{10... | collective-permute-start | bytes 786440
  479.0 33.9 %collective-permute-start.4 = (f32[16,4096]{1,0:T(8,128)S(1)}, f32[16,4096]{1,0:T(8,128)S(1)}, u32[]{:S(2)}, u32[]{:S(2)}) collective-permute-start(f32[16,4096]{1,0:T(8,128)S(1)} %fusion), channel_id=1, source_target_pairs={{0,4},{1,5},{2,6},{3,7},{4,8},{5,9},{6,10},{7,11},{8,12},{9,13},{1... | collective-permute-start | bytes 786440
  505.8 5.8 %copy-start.5 = (f32[14,4096]{1,0:T(8,128)}, f32[14,4096]{1,0:T(8,128)S(1)}, u32[]{:S(2)}) copy-start(f32[14,4096]{1,0:T(8,128)S(1)} %collective-permute-done.8) | copy-start | bytes 688132
  505.8 13.2 %collective-permute-start.5 = (f32[16,4096]{1,0:T(8,128)S(1)}, f32[16,4096]{1,0:T(8,128)S(1)}, u32[]{:S(2)}, u32[]{:S(2)}) collective-permute-start(f32[16,4096]{1,0:T(8,128)S(1)} %fusion), channel_id=1, source_target_pairs={{0,5},{1,6},{2,7},{3,8},{4,9},{5,10},{6,11},{7,12},{8,13},{9,14},{... | collective-permute-start | bytes 786440
  507.7 2.0 copy-start.3
  507.7 17.4 %collective-permute-start.6 = (f32[16,4096]{1,0:T(8,128)S(1)}, f32[16,4096]{1,0:T(8,128)S(1)}, u32[]{:S(2)}, u32[]{:S(2)}) collective-permute-start(f32[16,4096]{1,0:T(8,128)S(1)} %fusion), channel_id=1, source_target_pairs={{0,6},{1,7},{2,8},{3,9},{4,10},{5,11},{6,12},{7,13},{8,14},{9,15},... | collective-permute-start | bytes 786440
  509.7 2.0 copy-start.4
  509.7 21.2 %collective-permute-start.7 = (f32[16,4096]{1,0:T(8,128)S(1)}, f32[16,4096]{1,0:T(8,128)}, u32[]{:S(2)}, u32[]{:S(2)}) collective-permute-start(f32[16,4096]{1,0:T(8,128)S(1)} %fusion), channel_id=1, source_target_pairs={{0,7},{1,8},{2,9},{3,10},{4,11},{5,12},{6,13},{7,14},{8,15},{9,16}... | collective-permute-start | bytes 786440
  512.9 12.2 %copy-start.6 = (f32[16,4096]{1,0:T(8,128)}, f32[16,4096]{1,0:T(8,128)S(1)}, u32[]{:S(2)}) copy-start(f32[16,4096]{1,0:T(8,128)S(1)} %collective-permute-done.3) | copy-start | bytes 786436
  512.9 12.2 %copy-start.7 = (f32[16,4096]{1,0:T(8,128)}, f32[16,4096]{1,0:T(8,128)S(1)}, u32[]{:S(2)}) copy-start(f32[16,4096]{1,0:T(8,128)S(1)} %collective-permute-done.4) | copy-start | bytes 786436
  519.0 6.1 %copy-start.8 = (f32[16,4096]{1,0:T(8,128)}, f32[16,4096]{1,0:T(8,128)S(1)}, u32[]{:S(2)}) copy-start(f32[16,4096]{1,0:T(8,128)S(1)} %collective-permute-done.5) | copy-start | bytes 786436
  525.1 0.7 copy-start.9
Sparse Core Ops, SparseCore 0:
  11.7 102.5 all-gather.2
  128.2 131.3 all-gather.4
  299.6 131.1 all-reduce.3
where the time goes:
time: 560 us; the launch traced here: 559 us
  waiting for transfers between devices  270 us (48%)
  blocking collectives  172 us (31%)
  matrix products  51.4 us (9%)
  starting transfers between devices  24.3 us (4%)
  local copies, waits for them, and re-layouts  24.1 us (4%)
  between operations  14.7 us (3%)
    unnamed x1, blocking collectives  172 us
    all_gather x1, waiting for transfers between devices, coupling_term(): segment = lax.all_gather(centered, 'dp', axis=1, tiled=True)  131 us
    all_gather x1, waiting for transfers between devices, on_device(): gathered = lax.all_gather(hidden, 'dp', axis=1, tiled=True)  105 us
    unnamed x11, waiting for transfers between devices  34.2 us
    unnamed x28, local copies, waits for them, and re-layouts  24.1 us
    unnamed x8, starting transfers between devices  23.3 us
    dot_general x1, matrix products, on_device(): lax.dot_general(gathered[0], grad_embed, (((0,), (0,)), ((), ())), prefer...  14.8 us
    dot_general x1, matrix products, on_device(): jnp.dot(flat, weight, preferred_element_type=jnp.float32)  12.9 us
  transfers between devices with their start and end apart: 12, of which 6 were waited for; matrix products, arithmetic and copies ran while one was open for 36% of the time, Pallas kernels for 0%

commit v1 on v0

--- a/solution.py
+++ b/solution.py
@@ -21,7 +21,9 @@
 
 
 def coupling_term(centered):
-    segment = lax.all_gather(centered, "dp", axis=1, tiled=True)
+    segment = jnp.concatenate(
+        lax.all_to_all(jnp.stack([centered] * lax.axis_size("dp")), "dp", 0, 0), axis=1
+    )
     product_tile = lax.dot_general(
         centered, segment, (((0,), (0,)), ((), ())), preferred_element_type=jnp.float32
     )

time: 560 us -> 644 us (1.15)
  waiting for transfers between devices: 270 us -> 338 us
    all_to_all x0 -> x1, waiting for transfers between devices: none -> 199 us  [coupling_term(): lax.all_to_all(jnp.stack([centered] * lax.axis_size('dp')), 'dp', 0, 0)]
    all_gather x1 -> x0, waiting for transfers between devices: 131 us -> none  [coupling_term(): segment = lax.all_gather(centered, 'dp', axis=1, tiled=True)]
    another operation x0 -> x1, local copies, waits for them, and re-layouts: none -> 7.34 us  [coupling_term(): jnp.stack([centered] * lax.axis_size('dp'))]
    unnamed x28 -> x34, local copies, waits for them, and re-layouts: 24.1 us -> 22.7 us
    unnamed x11 -> x10, waiting for transfers between devices: 34.2 us -> 33.3 us
  transfers between devices with their start and end apart: 12 -> 12, of which waited for: 6 -> 6; matrix products, arithmetic and copies ran while one was open for 36% -> 32% of each run, Pallas kernels for 0% -> 0%
where the time goes in v1:
time: 644 us; the launch traced here: 643 us
  waiting for transfers between devices  338 us (52%)
  blocking collectives  172 us (27%)
  matrix products  55.1 us (9%)
  local copies, waits for them, and re-layouts  30.3 us (5%)
  starting transfers between devices  30.2 us (5%)
  between operations  15 us (2%)
    all_to_all x1, waiting for transfers between devices, coupling_term(): lax.all_to_all(jnp.stack([centered] * lax.axis_size('dp')), 'dp', 0, 0)  199 us
    unnamed x1, blocking collectives  172 us
    all_gather x1, waiting for transfers between devices, on_device(): gathered = lax.all_gather(hidden, 'dp', axis=1, tiled=True)  105 us
    unnamed x10, waiting for transfers between devices  33.3 us
    unnamed x34, local copies, waits for them, and re-layouts  22.7 us
    unnamed x8, starting transfers between devices  22.1 us
    dot_general x1, matrix products, on_device(): jnp.dot(flat, weight, preferred_element_type=jnp.float32)  12.9 us
  transfers between devices with their start and end apart: 12, of which 6 were waited for; matrix products, arithmetic and copies ran while one was open for 32% of the time, Pallas kernels for 0%

profile of v1, /device:TPU:8, one launch (start us, length us, event | category | flops | bytes accessed | tf_op | source)
XLA Modules:
  0.0 642.5 jit_solution(13297689659200285311)
XLA Ops:
  9.1 105.2 %all-gather.2.cloned.1.call-done = bf16[1,896,4096]{2,0,1:T(2,128)(2,1)} async-done(((bf16[1,14,4096]{2,0,1:T(2,128)(2,1)}), bf16[1,896,4096]{2,0,1:T(2,128)(2,1)}) %all-gather.2.cloned.1.call-update) | async-done | bytes 7340048 | tf_op jit(solution)/shard_map/all_gather | solution.py:67
  114.3 12.9 %convert_reduce_fusion = (f32[128]{0:T(128)S(1)}, bf16[896,128]{1,0:T(8,128)(2,1)S(1)}) fusion(bf16[4096,128]{1,0:T(8,128)(2,1)S(1)} %copy-done, bf16[1,896,4096]{2,0,1:T(2,128)(2,1)} %all-gather.2.cloned.1.call-done), kind=kOutput, calls=%fused_computation.20 | convolution fusion | flops 939868032 | bytes 8618496 | tf_op jit(solution)/shard_map/dot_general | solution.py:71
  127.6 7.3 %stack.4 = bf16[64,896,128]{1,2,0:T(8,128)(2,1)} broadcast(bf16[896,128]{0,1:T(8,128)(2,1)S(1)} %copy.14), dimensions={1,2} | broadcast | bytes 14909440 | tf_op jit(solution)/shard_map/stack | solution.py:25
  134.9 6.4 all-to-all-start
  143.1 199.0 %all-to-all-done = bf16[64,896,128]{1,2,0:T(8,128)(2,1)} async-done(((bf16[64,896,128]{1,2,0:T(8,128)(2,1)}), bf16[64,896,128]{1,2,0:T(8,128)(2,1)}, u32[]{:S(2)}, u32[]{:S(2)}) %all-to-all-start) | async-done | bytes 14680096 | tf_op jit(solution)/shard_map/all_to_all | solution.py:25
  342.1 10.0 %fusion.26 = f32[128,8192]{1,0:T(8,128)S(1)} fusion(bf16[896,8192]{0,1:T(8,128)(2,1)} %bitcast.3, bf16[896,128]{1,0:T(8,128)(2,1)S(1)} %get-tuple-element.15, f32[128]{0:T(128)S(1)} %broadcast_multiply_fusion.1), kind=kOutput, calls=%fused_computation.29 | convolution fusion | flops 1879392256 | bytes 19104256 | tf_op jit(solution)/shard_map/dot_general | solution.py:27
  352.1 7.4 %fusion.10 = f32[896,128]{1,0:T(8,128)S(1)} fusion(bf16[896,8192]{0,1:T(8,128)(2,1)} %bitcast.3, f32[128,8192]{1,0:T(8,128)S(1)} %fusion.26), kind=kOutput, calls=%fused_computation.8 | convolution fusion | flops 1883242496 | bytes 19333120 | tf_op jit(solution)/shard_map/dot_general | solution.py:33
  359.5 7.9 %fusion.20 = bf16[896,128]{1,0:T(8,128)(2,1)S(1)} fusion(bf16[896,128]{1,0:T(8,128)(2,1)S(1)} %get-tuple-element.15, bf16[1,896,128]{2,1,0:T(8,128)(2,1)S(1)} %collective-permute-done, f32[896,128]{1,0:T(8,128)S(1)} %fusion.10, bf16[896,8192]{0,1:T(8,128)(2,1)} %bitcast.3, f32[128,8192]{1,0:T(8,128)S(1)} %fusion.26, f32[128]{0:T(128)S(1)} %get-tuple-element.10, ...), kind=kOutput, calls=%fused_computation.24 | convolution fusion | flops 1881817088 | bytes 20023296 | tf_op jit(solution)/shard_map/dot_general | solution.py:32
  367.5 7.2 %fusion.28 = f32[896,4096]{1,0:T(8,128)} fusion(bf16[896,128]{1,0:T(8,128)(2,1)S(1)} %fusion.20, bf16[4096,128]{1,0:T(8,128)(2,1)S(1)} %copy-done), kind=kOutput, calls=%fused_computation.33 | convolution fusion | flops 939524096 | bytes 15958016 | tf_op jit(solution)/shard_map/dot_general | solution.py:55
  374.7 9.6 %fusion.5 = f32[4096,128]{0,1:T(8,128)} fusion(bf16[896,128]{1,0:T(8,128)(2,1)S(1)} %fusion.20, bf16[1,896,4096]{2,0,1:T(2,128)(2,1)S(1)} %bitcast.33), kind=kOutput, calls=%fused_computation.4 | convolution fusion | flops 939524096 | bytes 9666560 | tf_op jit(solution)/shard_map/dot_general | solution.py:76
  384.4 172.4 %fusion = f32[16,4096]{1,0:T(8,128)S(1)} fusion(f32[896,4096]{1,0:T(8,128)} %fusion.28), kind=kCustom, calls=%all-reduce-scatter | all-reduce-scatter fusion | flops 4194305 | bytes 14942720
  556.8 1.9 collective-permute-start.1
  558.7 1.9 collective-permute-start.2
  560.7 1.9 collective-permute-start.8
  562.6 1.9 collective-permute-start.3
  564.6 8.7 %collective-permute-start.4 = (f32[16,4096]{1,0:T(8,128)S(1)}, f32[16,4096]{1,0:T(8,128)S(1)}, u32[]{:S(2)}, u32[]{:S(2)}) collective-permute-start(f32[16,4096]{1,0:T(8,128)S(1)} %fusion), channel_id=1, source_target_pairs={{0,4},{1,5},{2,6},{3,7},{4,8},{5,9},{6,10},{7,11},{8,12},{9,13},{1... | collective-permute-start | bytes 786440
  573.2 16.3 %collective-permute-done.8 = f32[14,4096]{1,0:T(8,128)S(1)} collective-permute-done((f32[14,4096]{1,0:T(8,128)S(1)}, f32[14,4096]{1,0:T(8,128)S(1)}, u32[]{:S(2)}, u32[]{:S(2)}) %collective-permute-start.8) | collective-permute-done | bytes 229408
  589.5 1.9 collective-permute-start.5
  591.5 1.9 collective-permute-start.6
  593.4 1.9 collective-permute-start.7
  596.7 7.4 %collective-permute-done.5 = f32[16,4096]{1,0:T(8,128)S(1)} collective-permute-done((f32[16,4096]{1,0:T(8,128)S(1)}, f32[16,4096]{1,0:T(8,128)S(1)}, u32[]{:S(2)}, u32[]{:S(2)}) %collective-permute-start.5) | collective-permute-done | bytes 262176
  604.1 3.7 collective-permute-done.6
  608.5 5.9 collective-permute-done.7
  614.4 16.7 %concatenate = f32[142,4096]{1,0:T(8,128)S(1)} concatenate(f32[14,4096]{1,0:T(8,128)} %copy-done.4, f32[16,4096]{1,0:T(8,128)} %collective-permute-done.7, f32[16,4096]{1,0:T(8,128)} %copy-done.8, f32[16,4096]{1,0:T(8,128)} %copy-done.7, f32[16,4096]{1,0:T(8,128)} %copy-done.6, f32[16,4096]{1,0:T(8,128)} %copy-done.5, f32[16,4096]{1,0:T(8,128)} %copy-done.3, ...), dimensions={0} | concatenate | bytes 4653056
  (51 shorter events, 9.9 us)
Async XLA Ops:
  7.2 107.2 %copy-start = (bf16[4096,128]{1,0:T(8,128)(2,1)S(1)}, bf16[4096,128]{1,0:T(8,128)(2,1)}, u32[]{:S(2)}) copy-start(bf16[4096,128]{1,0:T(8,128)(2,1)} %param.3) | copy-start | bytes 3145732
  7.2 107.2 %all-gather.2.cloned.1.call-start = ((), (), s32[]{:S(2)}) async-start(), calls=%async_computation.1 | async-start | bytes 14909440 | tf_op jit(solution)/shard_map/all_gather | solution.py:67
  134.9 207.1 %all-to-all-start = ((bf16[64,896,128]{1,2,0:T(8,128)(2,1)}), bf16[64,896,128]{1,2,0:T(8,128)(2,1)}, u32[]{:S(2)}, u32[]{:S(2)}) async-start(bf16[64,896,128]{1,2,0:T(8,128)(2,1)} %stack.4), calls=%async_computation | async-start | bytes 29360128 | tf_op jit(solution)/shard_map/all_to_all | solution.py:25
  141.4 490.7 %all-reduce.4.cloned.1.call-start = ((), (), s32[]{:S(2)}) async-start(), calls=%async_computation.2 | async-start | bytes 4194304 | tf_op jit(solution)/shard_map/psum | solution.py:79
  141.4 218.0 %collective-permute-start = (bf16[1,896,128]{2,1,0:T(8,128)(2,1)S(1)}, bf16[1,896,128]{2,1,0:T(8,128)(2,1)S(1)}, u32[]{:S(2)}, u32[]{:S(2)}) collective-permute-start(bf16[1,896,128]{2,1,0:T(8,128)(2,1)S(1)} %bitcast.34), channel_id=1, source_target_pairs={{0,64},{64,0},{1,65},{65,1},{2,66},{66,2},{3,67},{67,3},{4,68},{68... | collective-permute-start | bytes 688136 | tf_op jit(solution)/shard_map/ppermute | solution.py:14
  359.5 15.2 %slice-start = ((s8[14680064]{0:T(1024)(128)(4,1)}), s8[4194304]{0:T(1024)(128)(4,1)S(1)}, s32[]{:S(2)}) async-start(s8[14680064]{0:T(1024)(128)(4,1)} %bitcast.32), calls=%async_computation.3 | async-start | bytes 8388608
  359.5 15.2 %slice-start.1 = ((s8[14680064]{0:T(1024)(128)(4,1)}), s8[4194304]{0:T(1024)(128)(4,1)S(1)}, s32[]{:S(2)}) async-start(s8[14680064]{0:T(1024)(128)(4,1)} %bitcast.32), calls=%async_computation.4 | async-start | bytes 8388608
  359.5 15.2 %slice-start.2 = ((s8[14680064]{0:T(1024)(128)(4,1)}), s8[2097152]{0:T(1024)(128)(4,1)S(1)}, s32[]{:S(2)}) async-start(s8[14680064]{0:T(1024)(128)(4,1)} %bitcast.32), calls=%async_computation.5 | async-start | bytes 4194304
  367.5 7.2 %slice-start.3 = ((s8[14680064]{0:T(1024)(128)(4,1)}), s8[4194304]{0:T(1024)(128)(4,1)S(1)}, s32[]{:S(2)}) async-start(s8[14680064]{0:T(1024)(128)(4,1)} %bitcast.32), calls=%async_computation.6 | async-start | bytes 8388608
  384.4 211.0 %copy-start.9 = (u32[128]{0:T(128)S(1)}, u32[128]{0:T(128)}, u32[]{:S(2)}) copy-start(u32[128]{0:T(128)} %constant.24) | copy-start | bytes 1540
  556.8 51.0 %copy-start.1 = (f32[16,4096]{1,0:T(8,128)}, f32[16,4096]{1,0:T(8,128)S(1)}, u32[]{:S(2)}) copy-start(f32[16,4096]{1,0:T(8,128)S(1)} %fusion) | copy-start | bytes 786436
  556.8 34.7 %collective-permute-start.1 = (f32[16,4096]{1,0:T(8,128)S(1)}, f32[16,4096]{1,0:T(8,128)S(1)}, u32[]{:S(2)}, u32[]{:S(2)}) collective-permute-start(f32[16,4096]{1,0:T(8,128)S(1)} %fusion), channel_id=1, source_target_pairs={{0,1},{1,2},{2,3},{3,4},{4,5},{5,6},{6,7},{7,8},{8,9},{9,10},{10,1... | collective-permute-start | bytes 786440
  558.7 34.7 %collective-permute-start.2 = (f32[16,4096]{1,0:T(8,128)S(1)}, f32[16,4096]{1,0:T(8,128)S(1)}, u32[]{:S(2)}, u32[]{:S(2)}) collective-permute-start(f32[16,4096]{1,0:T(8,128)S(1)} %fusion), channel_id=1, source_target_pairs={{0,2},{1,3},{2,4},{3,5},{4,6},{5,7},{6,8},{7,9},{8,10},{9,11},{10,... | collective-permute-start | bytes 786440
  560.7 28.8 %collective-permute-start.8 = (f32[14,4096]{1,0:T(8,128)S(1)}, f32[14,4096]{1,0:T(8,128)S(1)}, u32[]{:S(2)}, u32[]{:S(2)}) collective-permute-start(f32[14,4096]{1,0:T(8,128)S(1)} %slice), channel_id=1, source_target_pairs={{0,8},{1,9},{2,10},{3,11},{4,12},{5,13},{6,14},{7,15},{8,16},{9,17... | collective-permute-start | bytes 688136
  562.6 34.0 %collective-permute-start.3 = (f32[16,4096]{1,0:T(8,128)S(1)}, f32[16,4096]{1,0:T(8,128)S(1)}, u32[]{:S(2)}, u32[]{:S(2)}) collective-permute-start(f32[16,4096]{1,0:T(8,128)S(1)} %fusion), channel_id=1, source_target_pairs={{0,3},{1,4},{2,5},{3,6},{4,7},{5,8},{6,9},{7,10},{8,11},{9,12},{10... | collective-permute-start | bytes 786440
  564.6 32.1 %collective-permute-start.4 = (f32[16,4096]{1,0:T(8,128)S(1)}, f32[16,4096]{1,0:T(8,128)S(1)}, u32[]{:S(2)}, u32[]{:S(2)}) collective-permute-start(f32[16,4096]{1,0:T(8,128)S(1)} %fusion), channel_id=1, source_target_pairs={{0,4},{1,5},{2,6},{3,7},{4,8},{5,9},{6,10},{7,11},{8,12},{9,13},{1... | collective-permute-start | bytes 786440
  589.5 5.8 copy-start.4
  589.5 14.6 %collective-permute-start.5 = (f32[16,4096]{1,0:T(8,128)S(1)}, f32[16,4096]{1,0:T(8,128)S(1)}, u32[]{:S(2)}, u32[]{:S(2)}) collective-permute-start(f32[16,4096]{1,0:T(8,128)S(1)} %fusion), channel_id=1, source_target_pairs={{0,5},{1,6},{2,7},{3,8},{4,9},{5,10},{6,11},{7,12},{8,13},{9,14},{... | collective-permute-start | bytes 786440
  591.5 16.3 %collective-permute-start.6 = (f32[16,4096]{1,0:T(8,128)S(1)}, f32[16,4096]{1,0:T(8,128)S(1)}, u32[]{:S(2)}, u32[]{:S(2)}) collective-permute-start(f32[16,4096]{1,0:T(8,128)S(1)} %fusion), channel_id=1, source_target_pairs={{0,6},{1,7},{2,8},{3,9},{4,10},{5,11},{6,12},{7,13},{8,14},{9,15},... | collective-permute-start | bytes 786440
  593.4 2.0 copy-start.3
  593.4 20.9 %collective-permute-start.7 = (f32[16,4096]{1,0:T(8,128)S(1)}, f32[16,4096]{1,0:T(8,128)}, u32[]{:S(2)}, u32[]{:S(2)}) collective-permute-start(f32[16,4096]{1,0:T(8,128)S(1)} %fusion), channel_id=1, source_target_pairs={{0,7},{1,8},{2,9},{3,10},{4,11},{5,12},{6,13},{7,14},{8,15},{9,16}... | collective-permute-start | bytes 786440
  596.7 11.1 %copy-start.5 = (f32[16,4096]{1,0:T(8,128)}, f32[16,4096]{1,0:T(8,128)S(1)}, u32[]{:S(2)}) copy-start(f32[16,4096]{1,0:T(8,128)S(1)} %collective-permute-done.3) | copy-start | bytes 786436
  596.7 11.1 %copy-start.6 = (f32[16,4096]{1,0:T(8,128)}, f32[16,4096]{1,0:T(8,128)S(1)}, u32[]{:S(2)}) copy-start(f32[16,4096]{1,0:T(8,128)S(1)} %collective-permute-done.4) | copy-start | bytes 786436
  604.1 3.7 copy-start.7
  (2 other events, 2.7 us)
Sparse Core Ops, SparseCore 0:
  11.7 102.5 all-gather.1
  384.5 137.7 all-reduce.3
